TPU v7x, 128 devices: a whole 4x4x4 slice. The times are simulated.
128 devices in a mesh: seq: 8 (over y_lo, z), wide: 16 (over x, y_hi, core).
Axes of the slice: x: 4, y: 4 (y_hi: 2, y_lo: 2; y = y_hi * 2 + y_lo), z: 4, core: 2. Of those that a mesh axis runs over, the one named last changes fastest.
Arguments:
- activations: bfloat16 [8, 5120], P(None, 'wide'), may hold values from -6 to 6
- attn_gain: float32 [5120], P('wide'), may hold values from 0.25 to 1.75
- w_query: bfloat16 [5120, 8192], P('wide', 'seq'), may hold values from -0.078125 to 0.078125
- w_keyval: bfloat16 [5120, 2, 1024], P('wide', None, 'seq'), may hold values from -0.078125 to 0.078125
- w_output: bfloat16 [8192, 5120], P('seq', 'wide'), may hold values from -0.0625 to 0.0625
- query_gain: float32 [128], replicated, may hold values from 1.5 to 3
- key_gain: float32 [128], replicated, may hold values from 1.5 to 3
- key_cache: bfloat16 [8, 65536, 8, 128], P(None, ('seq', 'wide')), may hold values from -400 to 400
- value_cache: bfloat16 [8, 65536, 8, 128], P(None, ('seq', 'wide')), may hold values from -6 to 6
- lengths: int32 [8], replicated, may hold values from 8192 to 65536, as said below
Outputs:
- attended: float32 [8, 5120], P(None, 'wide')
Inputs may be any that keep to these rules, and one draw needn't show every extreme that they name: `lengths`: some sequence has exactly 65536 valid positions.
All inputs are finite; a program needn't handle non-finite values.
Results may differ from a plain program's by a relative error of at most 0.014.
The roundings to bfloat16 on the way count: a program that leaves them out, or rounds other values in their place, can miss the bound.
Values may be sent and summed in bfloat16 or wider, within the bound.
A program may use at most 128 MiB of HBM per device.

v0:
```python
import math

import jax
import jax.numpy as jnp
from jax import lax
from jax.sharding import PartitionSpec as P

rope_base = 1000000.0
eps_norm = 1e-06
neg_large = -1e30


def joined(shard, axis, combine):
    everything = jax.tree.map(lambda part: lax.all_gather(part, axis), shard)
    leading = jax.tree.map(lambda part: part[0], everything)

    def lap(k, so_far):
        return combine(so_far, jax.tree.map(lambda part: part[k], everything))

    return lax.fori_loop(1, lax.axis_size(axis), lap, leading)


def rotate_pos(vector, positions):
    half = vector.shape[-1] // 2
    freq_index = jnp.arange(half, dtype=jnp.float32)
    inverse_freq = jnp.exp(-(2.0 * freq_index / vector.shape[-1]) * math.log(rope_base))
    angles = positions.astype(jnp.float32)[:, None, None] * inverse_freq
    cosine = jnp.cos(angles)
    sine = jnp.sin(angles)
    first_half = vector[..., :half]
    second_half = vector[..., half:]
    return jnp.concatenate(
        [first_half * cosine - second_half * sine, second_half * cosine + first_half * sine],
        axis=-1,
    )


def head_norm(vector, gain):
    return vector * lax.rsqrt(jnp.mean(vector * vector, axis=-1, keepdims=True) + eps_norm) * gain


def combine(earlier, later):
    peak_a, total_a, numer_a = earlier
    peak_b, total_b, numer_b = later
    peak_top = jnp.maximum(peak_a, peak_b)
    factor_a = jnp.exp(peak_a - peak_top)
    factor_b = jnp.exp(peak_b - peak_top)
    return (
        peak_top,
        total_a * factor_a + total_b * factor_b,
        numer_a * factor_a[..., None] + numer_b * factor_b[..., None],
    )


def body(
    activations,
    attn_gain,
    w_query,
    w_keyval,
    w_output,
    query_gain,
    key_gain,
    key_cache,
    value_cache,
    lengths,
):
    row_count = activations.shape[0]
    width_dev = activations.shape[1]
    head_dim = query_gain.shape[0]
    x_float = activations.astype(jnp.float32)
    square_sum = jnp.sum(x_float * x_float, axis=-1)
    normed = (x_float * attn_gain).astype(jnp.bfloat16)
    part_query = jnp.dot(normed, w_query, preferred_element_type=jnp.float32)
    part_keyval = jnp.dot(
        normed, w_keyval.reshape(width_dev, -1), preferred_element_type=jnp.float32
    )
    square_sum, part_query, part_keyval = lax.psum((square_sum, part_query, part_keyval), "wide")
    inv_rms = lax.rsqrt(square_sum / (width_dev * lax.axis_size("wide")) + eps_norm)
    heads_dev = part_query.shape[1] // head_dim
    kv_dev = part_keyval.shape[1] // (2 * head_dim)
    query_rows = (part_query * inv_rms[:, None]).reshape(row_count, heads_dev, head_dim)
    query_rows = (
        rotate_pos(head_norm(query_rows, query_gain), lengths)
        .astype(jnp.bfloat16)
        .reshape(row_count, -1)
    )
    keyval = (part_keyval * inv_rms[:, None]).reshape(row_count, 2, kv_dev, head_dim)
    key_fresh = (
        rotate_pos(head_norm(keyval[:, 0], key_gain), lengths)
        .astype(jnp.bfloat16)
        .reshape(row_count, -1)
    )
    value_fresh = keyval[:, 1].astype(jnp.bfloat16).reshape(row_count, -1)
    query_all, key_all, value_all = (
        lax.all_gather(query_rows, "seq", axis=1, tiled=True),
        lax.all_gather(key_fresh, "seq", axis=1, tiled=True),
        lax.all_gather(value_fresh, "seq", axis=1, tiled=True),
    )
    kv_heads = key_cache.shape[2]
    group_size = query_all.shape[1] // head_dim // kv_heads
    grouped = query_all.reshape(row_count, kv_heads, group_size, head_dim)
    score_scale = head_dim ** (-0.5)
    block_len = key_cache.shape[1]
    block_index = lax.axis_index("seq") * lax.axis_size("wide") + lax.axis_index("wide")
    positions = block_index * block_len + jnp.arange(block_len, dtype=jnp.int32)
    in_cache = (positions[None, :] < lengths[:, None])[:, None, None, :]
    scores = (
        jnp.einsum("bgjd,btgd->bgjt", grouped, key_cache, preferred_element_type=jnp.float32)
        * score_scale
    )
    scores = jnp.where(in_cache, scores, neg_large)
    key_heads = key_all.reshape(row_count, kv_heads, head_dim)
    fresh_score = (
        jnp.einsum("bgjd,bgd->bgj", grouped, key_heads, preferred_element_type=jnp.float32)
        * score_scale
    )
    anchor = block_index == 0
    peak_score = jnp.maximum(jnp.max(scores, axis=-1), jnp.where(anchor, fresh_score, neg_large))
    weights = jnp.where(in_cache, jnp.exp(scores - peak_score[..., None]), 0.0)
    fresh_weight = jnp.where(anchor, jnp.exp(fresh_score - peak_score), 0.0)
    row_total = jnp.sum(weights, axis=-1) + fresh_weight
    numerator = jnp.einsum(
        "bgjt,btgd->bgjd",
        weights.astype(jnp.bfloat16),
        value_cache,
        preferred_element_type=jnp.float32,
    )
    value_heads = value_all.reshape(row_count, kv_heads, 1, head_dim).astype(jnp.float32)
    numerator = (
        numerator + fresh_weight.astype(jnp.bfloat16).astype(jnp.float32)[..., None] * value_heads
    )
    own_groups = kv_heads // lax.axis_size("seq")
    start = lax.axis_index("seq") * own_groups
    merged = joined((peak_score, row_total, numerator), ("seq", "wide"), combine)
    own_total = lax.dynamic_slice_in_dim(merged[1], start, own_groups, 1)
    own_numer = lax.dynamic_slice_in_dim(merged[2], start, own_groups, 1)
    attended_heads = (own_numer / own_total[..., None]).astype(jnp.bfloat16).reshape(row_count, -1)
    partial_value = jnp.dot(attended_heads, w_output, preferred_element_type=jnp.float32)
    return lax.psum(partial_value, "seq")


def solution(mesh):
    return jax.shard_map(
        body,
        mesh=mesh,
        in_specs=(
            P(None, "wide"),
            P("wide"),
            P("wide", "seq"),
            P("wide", None, "seq"),
            P("seq", "wide"),
            P(),
            P(),
            P(None, ("seq", "wide"), None, None),
            P(None, ("seq", "wide"), None, None),
            P(),
        ),
        out_specs=P(None, "wide"),
        check_vma=False,
    )
```

profile of v0, /device:TPU:0, one launch (start us, length us, event | category | flops | bytes accessed | tf_op | source)
XLA Modules:
  0.0 841.3 jit_solution(5087205885458228187)
XLA Ops:
  9.4 69.8 %all-reduce = (f32[8,1024]{1,0:T(8,128)S(1)}, f32[8]{0:T(128)S(1)}, f32[8,256]{1,0:T(8,128)S(1)}) all-reduce(f32[8,1024]{1,0:T(8,128)S(1)} %fusion.45, f32[8]{0:T(128)S(1)} %fusion.38, f32[8,256]{1,0:T(8,128)S(1)} %fusion.22), channel_id=1, replica_groups=mesh['seq'=8,'wide'=16] {'wide'}, use_global_device_ids=true, to_apply=%region_0.0 | all-reduce | flops 10248 | bytes 81984 | tf_op jit(solution)/shard_map/psum | solution.py:77
  82.7 24.2 %all_gather.28 = bf16[8,1024]{1,0:T(8,128)(2,1)S(1)} all-gather(bf16[8,128]{1,0:T(8,128)(2,1)S(1)} %pad_maximum_fusion), channel_id=1, replica_groups=mesh['seq'=8,'wide'=16] {'seq'}, dimensions={1}, use_global_device_ids=true | all-gather | bytes 18432 | tf_op jit(solution)/shard_map/all_gather | solution.py:96
  106.8 23.6 %all-gather.2 = bf16[8,1,1,1024]{3,0,1,2:T(8,128)(2,1)S(1)} all-gather(bf16[8,1,1,128]{3,0,1,2:T(8,128)(2,1)S(1)} %slice.69), channel_id=4, replica_groups=mesh['seq'=8,'wide'=16] {'seq'}, dimensions={3}, use_global_device_ids=true | all-gather | bytes 18432 | tf_op jit(solution)/shard_map/all_gather | solution.py:97
  131.4 28.2 %all_gather.27 = bf16[8,8192]{1,0:T(8,128)(2,1)S(1)} all-gather(bf16[8,1024]{1,0:T(8,128)(2,1)S(1)} %maximum_bitcast_fusion), channel_id=1, replica_groups=mesh['seq'=8,'wide'=16] {'seq'}, dimensions={1}, use_global_device_ids=true | all-gather | bytes 147456 | tf_op jit(solution)/shard_map/all_gather | solution.py:95
  159.8 5.8 fusion.55
  165.9 2.3 fusion.13
  168.3 182.8 %all-gather = f32[1024,8,8]{2,1,0:T(8,128)S(1)} all-gather(f32[8,8,8]{2,1,0:T(8,128)S(1)} %select_maximum_fusion), channel_id=2, replica_groups=mesh['seq'=8,'wide'=16] {'seq','wide'}, dimensions={0}, use_global_device_ids=true | all-gather | bytes 264192 | tf_op jit(solution)/shard_map/all_gather | solution.py:14
  351.1 2.0 copy-done.2
  353.1 186.4 %all-gather.1 = f32[1024,8,8]{2,1,0:T(8,128)S(1)} all-gather(f32[8,8,8]{2,1,0:T(8,128)S(1)} %get-tuple-element.206), channel_id=3, replica_groups=mesh['seq'=8,'wide'=16] {'seq','wide'}, dimensions={0}, use_global_device_ids=true | all-gather | bytes 264192 | tf_op jit(solution)/shard_map/all_gather | solution.py:14
  539.5 1.9 copy-done.3
  542.4 260.9 %while.19 = (s32[]{:T(128)}, f32[8,8,8]{2,1,0:T(8,128)S(1)}, f32[8,8,8]{2,1,0:T(8,128)S(1)}, f32[8,8,8,128]{3,2,1,0:T(8,128)S(1)}, f32[128,8,8,8]{3,2,1,0:T(8,12...) while((s32[]{:T(128)}, f32[8,8,8]{2,1,0:T(8,128)S(1)}, ...), condition=%wide.region_9.10_spmd, body=%wide.region_8.9_spmd.sunk | while | flops 199685 | bytes 807055 | solution.py:20
  543.3 1.2 fusion.61
  547.4 1.2 fusion.61
  551.5 1.2 fusion.61
  555.6 1.2 fusion.61
  559.7 1.2 fusion.61
  563.8 1.2 fusion.61
  567.9 1.2 fusion.61
  572.0 1.2 fusion.61
  576.1 1.2 fusion.61
  578.2 1.2 fusion.61
  582.3 1.2 fusion.61
  586.4 1.2 fusion.61
  590.5 1.2 fusion.61
  594.6 1.2 fusion.61
  598.7 1.2 fusion.61
  602.8 1.2 fusion.61
  607.0 1.2 fusion.61
  611.1 1.2 fusion.61
  615.2 1.2 fusion.61
  617.2 1.2 fusion.61
  621.3 1.2 fusion.61
  625.4 1.2 fusion.61
  629.6 1.2 fusion.61
  633.7 1.2 fusion.61
  637.8 1.2 fusion.61
  641.9 1.2 fusion.61
  646.0 1.2 fusion.61
  650.1 1.2 fusion.61
  654.2 1.2 fusion.61
  656.3 1.2 fusion.61
  660.4 1.2 fusion.61
  664.5 1.2 fusion.61
  668.6 1.2 fusion.61
  672.7 1.2 fusion.61
  676.8 1.2 fusion.61
  680.9 1.2 fusion.61
  685.0 1.2 fusion.61
  689.1 1.2 fusion.61
  693.2 1.2 fusion.61
  695.3 1.2 fusion.61
  699.4 1.2 fusion.61
  703.5 1.2 fusion.61
  707.6 1.2 fusion.61
  711.7 1.2 fusion.61
  715.8 1.2 fusion.61
  719.9 1.2 fusion.61
  724.0 1.2 fusion.61
  728.2 1.2 fusion.61
  732.3 1.2 fusion.61
  734.3 1.2 fusion.61
  738.4 1.2 fusion.61
  742.5 1.2 fusion.61
  803.8 30.7 %psum.31 = f32[8,320]{1,0:T(8,128)} all-reduce(f32[8,320]{1,0:T(8,128)S(1)} %fusion.33), channel_id=1, replica_groups=mesh['seq'=8,'wide'=16] {'seq'}, use_global_device_ids=true, to_apply=%region_10.11 | all-reduce | flops 2560 | bytes 20480 | tf_op jit(solution)/shard_map/psum | solution.py:139
  (247 shorter events, 203.9 us)
Async XLA Ops:
  6.5 2.0 copy-start
  6.5 534.9 %all-gather.6.cloned.1.call-start = ((), (), s32[]{:S(2)}) async-start(), calls=%async_computation | async-start | bytes 33816576 | tf_op jit(solution)/shard_map/all_gather | solution.py:14
  79.4 86.5 %copy-start.1 = (bf16[8,512,8,128]{3,2,1,0:T(8,128)(2,1)S(1)}, bf16[8,512,8,128]{3,2,1,0:T(8,128)(2,1)}, u32[]{:S(2)}) copy-start(bf16[8,512,8,128]{3,2,1,0:T(8,128)(2,1)} %param.20) | copy-start | bytes 25165828
  168.3 635.2 %copy-start.4 = (bf16[1024,320]{0,1:T(8,128)(2,1)S(1)}, bf16[1024,320]{0,1:T(8,128)(2,1)}, u32[]{:S(2)}) copy-start(bf16[1024,320]{0,1:T(8,128)(2,1)} %param.16) | copy-start | bytes 1966084
  351.1 2.0 copy-start.2
  539.5 1.9 copy-start.3
Sparse Core Ops, SparseCore 0:
  168.4 269.7 all-gather.5
where the time goes:
time: 854 us; the launch traced here: 841 us
  blocking collectives  546 us (64%)
  other arithmetic  263 us (31%)
  between operations  13.5 us (2%)
  matrix products  10.6 us (1%)
    all_gather x2, blocking collectives, joined(): everything = jax.tree.map(lambda part: lax.all_gather(part, axis), shard)  369 us
    add x127, other arithmetic, combine(): numer_a * factor_a[..., None] + numer_b * factor_b[..., None]  154 us
    add x127, other arithmetic, combine(): total_a * factor_a + total_b * factor_b  104 us
    psum x1, blocking collectives, body(): lax.psum((square_sum, part_query, part_keyval), 'wide')  69.8 us
    psum x1, blocking collectives, body(): return lax.psum(partial_value, 'seq')  30.7 us
    all_gather x1, blocking collectives, body(): lax.all_gather(query_rows, 'seq', axis=1, tiled=True)  28.2 us
    all_gather x1, blocking collectives, body(): lax.all_gather(key_fresh, 'seq', axis=1, tiled=True)  24.2 us
    all_gather x1, blocking collectives, body(): lax.all_gather(value_fresh, 'seq', axis=1, tiled=True)  23.6 us
  transfers between devices with their start and end apart: 1, of which 0 were waited for; matrix products, arithmetic and copies ran while one was open for 0% of the time, Pallas kernels for 0%

commit v1 on v0

v1 whole, which is shorter than its diff:
```python
import math

import jax
import jax.numpy as jnp
import numpy as np
from jax import lax
from jax.experimental import pallas as pl
from jax.experimental.pallas import tpu as pltpu
from jax.sharding import PartitionSpec as P

rope_base = 1000000.0
eps_norm = 1e-06
neg_large = -1e30
MESH = pl.DeviceIdType.MESH
f32 = jnp.float32
bf16 = jnp.bfloat16

ROWS, KVH, GROUP, HD = 8, 8, 8, 128
HEADS = KVH * GROUP
BLOCK = 512
FLAT = BLOCK * KVH
CHUNK = 512
CHUNKS = FLAT // CHUNK
NSEQ, NWIDE = 8, 16
WIDTH = 320
D = 5120


def lane_iota(shape):
    return lax.broadcasted_iota(jnp.int32, shape, len(shape) - 1)


def kernel(
    x_hbm, gain_hbm, wq_hbm, wkv_hbm, wo_hbm, qg_hbm, kg_hbm, k_hbm, v_hbm, freq_hbm, len_ref,
    out_ref,
    x_v, gain_v, wq_v, wkv_v, wo_v, qg_v, kg_v, k_v, v_v, freq_v,
    s1, r1, skv, rkv, sq, qall, qf, qt, knew, vnew, scr, mst, lst, numf,
    s3n, s3t, r3n, r3t, s4n, s4t, r4n, r4t, of, s5, r5,
    in_sem, k_sem, v_sem, ssem, rsem,
):
    s = lax.axis_index("seq")
    w = lax.axis_index("wide")
    x = w // 4
    yh = (w // 2) % 2
    core = w % 2
    yl = s // 4
    z = s % 4

    small = [
        pltpu.make_async_copy(a, b, in_sem.at[i])
        for i, (a, b) in enumerate(
            [
                (x_hbm, x_v),
                (gain_hbm, gain_v),
                (wq_hbm, wq_v),
                (qg_hbm, qg_v),
                (kg_hbm, kg_v),
                (freq_hbm, freq_v),
                (wkv_hbm, wkv_v),
                (wo_hbm, wo_v),
            ]
        )
    ]
    for c in small[:6]:
        c.start()

    wide_to = []
    for kx in (2, 1, 3, 0):
        for ky in (1, 0):
            for kc in (0, 1):
                if kx or ky or kc:
                    wide_to.append(((x + kx) % 4) * 4 + ((yh + ky) % 2) * 2 + (core + kc) % 2)
    plane_to = []
    for kz in (2, 1, 3, 0):
        for ky in (1, 0):
            for kh in (1, 0):
                for kc in (0, 1):
                    if kz or ky or kh or kc:
                        plane_to.append(
                            (
                                ((yl + ky) % 2) * 4 + (z + kz) % 4,
                                x * 4 + ((yh + kh) % 2) * 2 + (core + kc) % 2,
                                bool(kz or ky),
                            )
                        )
    seq_to = []
    for kz in (2, 1, 3, 0):
        for ky in (1, 0):
            if kz or ky:
                seq_to.append(((yl + ky) % 2) * 4 + (z + kz) % 4)

    bar = pltpu.get_barrier_semaphore()
    n_bar = 0
    for tw in wide_to:
        pl.semaphore_signal(bar, inc=1, device_id=(s, tw), device_id_type=MESH)
        n_bar += 1
    for ts, tw, far in plane_to:
        if far:
            pl.semaphore_signal(bar, inc=1, device_id=(ts, tw), device_id_type=MESH)
            n_bar += 1

    for c in small[6:]:
        c.start()
    k_cp = [pltpu.make_async_copy(k_hbm.at[b], k_v.at[b], k_sem.at[b]) for b in range(ROWS)]
    v_cp = [pltpu.make_async_copy(v_hbm.at[b], v_v.at[b], v_sem.at[b]) for b in range(ROWS)]
    for c in k_cp + v_cp:
        c.start()

    def remote(src, dst, i, to):
        return pltpu.make_async_remote_copy(
            src_ref=src, dst_ref=dst, send_sem=ssem.at[i], recv_sem=rsem.at[i],
            device_id=to, device_id_type=MESH,
        )

    for c in small[:6]:
        c.wait()
    xf = x_v[...].astype(f32)
    ss = jnp.sum(xf * xf, axis=-1, keepdims=True)
    normed = (xf * gain_v[...][None, :]).astype(bf16)
    for p in range(4):
        part = jnp.dot(normed, wq_v[:, p * 256 : (p + 1) * 256], preferred_element_type=f32)
        s1[p, 0] = part[:, :HD]
        s1[p, 1] = part[:, HD:]
        s1[p, 2] = jnp.broadcast_to(ss, (ROWS, HD))
    r1[w] = s1[w % 4]

    pl.semaphore_wait(bar, n_bar)
    for tw in wide_to:
        remote(s1.at[tw % 4], r1.at[w], 0, (s, tw)).start()

    small[6].wait()
    row_i = lax.broadcasted_iota(jnp.int32, (WIDTH, 2 * WIDTH), 0)
    col_i = lax.broadcasted_iota(jnp.int32, (WIDTH, 2 * WIDTH), 1)
    spread = jnp.where(col_i // 2 == row_i, 1.0, 0.0).astype(bf16)
    twice = jnp.dot(normed, spread, preferred_element_type=f32)
    odd = lane_iota((ROWS, 2 * WIDTH)) % 2
    both = jnp.concatenate(
        [jnp.where(odd == 0, twice, 0.0), jnp.where(odd == 1, twice, 0.0)], axis=0
    ).astype(bf16)
    kv_part = jnp.dot(both, wkv_v[...], preferred_element_type=f32)
    skv[0] = kv_part[:ROWS]
    skv[1] = kv_part[ROWS:]
    for t in range(2):

        @pl.when(w != t)
        def _():
            remote(skv, rkv.at[w], 1, (s, t)).start()

        @pl.when(w == t)
        def _():
            rkv[w] = skv[...]

    row = lax.broadcasted_iota(jnp.int32, (ROWS, HD), 0)
    lane = lane_iota((ROWS, HD))
    lens = jnp.zeros((ROWS, HD), jnp.int32)
    for b in range(ROWS):
        lens = jnp.where(row == b, len_ref[b], lens)
    angle = lens.astype(f32) * freq_v[...]
    cosine = jnp.cos(angle)
    sine = jnp.where(lane < HD // 2, -jnp.sin(angle), jnp.sin(angle))

    def head(u, gain):
        u = u * lax.rsqrt(jnp.mean(u * u, axis=-1, keepdims=True) + eps_norm) * gain
        return u * cosine + pltpu.roll(u, HD // 2, 1) * sine

    remote(r1.at[pl.ds(0, NWIDE - 1)], r1.at[pl.ds(0, NWIDE - 1)], 0, (s, w)).wait_recv()
    tot = r1[0]
    for i in range(1, NWIDE):
        tot = tot + r1[i]
    inv_rms = lax.rsqrt(tot[2] / D + eps_norm)
    sq[...] = jnp.concatenate(
        [head(tot[0] * inv_rms, qg_v[...]), head(tot[1] * inv_rms, qg_v[...])], axis=0
    ).astype(bf16)

    p_own = w % 4
    for ts, tw, _far in plane_to:
        remote(sq, qall.at[s * 4 + p_own], 2, (ts, tw)).start()
    qall[s * 4 + p_own] = sq[...]

    @pl.when(w < 2)
    def _():
        remote(rkv.at[pl.ds(0, NWIDE - 1)], rkv.at[pl.ds(0, NWIDE - 1)], 1, (s, w)).wait_recv()
        kv = rkv[0]
        for i in range(1, NWIDE):
            kv = kv + rkv[i]
        knew[...] = head(kv[0] * inv_rms, kg_v[...]).astype(bf16).astype(f32)
        vnew[...] = (kv[1] * inv_rms).astype(bf16).astype(f32)

    remote(qall.at[pl.ds(0, 31)], qall.at[pl.ds(0, 31)], 2, (s, w)).wait_recv()
    qf[...] = qall[...].reshape(HEADS * ROWS, HD).astype(f32)
    for b in range(ROWS):
        qt[b] = qf[pl.ds(b, HEADS, stride=ROWS), :]

    scale = HD ** (-0.5)
    start = (s * NWIDE + w) * BLOCK
    clane = lane_iota((GROUP, CHUNK))
    bit0 = clane % 2 == 1
    bit1 = (clane // 2) % 2 == 1
    bit2 = (clane // 4) % 2 == 1
    of_group = [clane % KVH == g for g in range(KVH)]

    def attend(b, carry):
        q = qt[b].astype(bf16)
        limit = (len_ref[b] - start) * KVH
        peak = jnp.full((GROUP, CHUNK), neg_large, f32)
        for ch in range(CHUNKS):
            keys = k_v[b, pl.ds(ch * CHUNK, CHUNK), :]
            sc = lax.dot_general(q, keys, (((1,), (1,)), ((), ())), preferred_element_type=f32)
            g = [sc[i * GROUP : (i + 1) * GROUP] for i in range(KVH)]
            g = [jnp.where(bit0, g[i + 1], g[i]) for i in range(0, 8, 2)]
            g = [jnp.where(bit1, g[i + 1], g[i]) for i in range(0, 4, 2)]
            t = jnp.where(bit2, g[1], g[0]) * scale
            t = jnp.where(clane + ch * CHUNK < limit, t, neg_large)
            scr[ch] = t
            peak = jnp.maximum(peak, t)
        m = jnp.maximum(
            jnp.maximum(peak[:, 0:128], peak[:, 128:256]),
            jnp.maximum(peak[:, 256:384], peak[:, 384:512]),
        )
        for sh in (64, 32, 16, 8):
            m = jnp.maximum(m, pltpu.roll(m, sh, 1))
        m4 = jnp.concatenate([m, m, m, m], axis=1)
        total = jnp.zeros((GROUP, CHUNK), f32)
        num = jnp.zeros((HEADS, HD), f32)
        for ch in range(CHUNKS):
            e = jnp.exp(scr[ch] - m4)
            e = jnp.where(clane + ch * CHUNK < limit, e, 0.0)
            total = total + e
            wide_e = jnp.concatenate(
                [jnp.where(of_group[g], e, 0.0) for g in range(KVH)], axis=0
            ).astype(bf16)
            num = num + jnp.dot(
                wide_e, v_v[b, pl.ds(ch * CHUNK, CHUNK), :], preferred_element_type=f32
            )
        tl = total[:, 0:128] + total[:, 128:256] + total[:, 256:384] + total[:, 384:512]
        for sh in (64, 32, 16, 8):
            tl = tl + pltpu.roll(tl, sh, 1)
        mst[b] = m
        lst[b] = tl
        numf[b] = num.reshape(KVH, GROUP, HD)
        return carry

    block32 = lane // 32
    low16 = lane % 32 < 16

    def by_block(parts):
        out = parts[0]
        for i in range(1, 4):
            out = jnp.where(block32 == i, parts[i], out)
        return out

    slot3 = s * 2 + core
    for c in range(2):
        for b in range(c * 4, c * 4 + 4):
            k_cp[b].wait()
            v_cp[b].wait()
        lax.fori_loop(c * 4, c * 4 + 4, attend, 0)
        s3t[c] = jnp.where(
            low16,
            by_block([mst[c * 4 + i] for i in range(4)]),
            by_block([lst[c * 4 + i] for i in range(4)]),
        )
        for g in range(KVH):
            s3n[c, g] = jnp.concatenate([numf[c * 4 + i, g] for i in range(4)], axis=0).astype(bf16)
        tw = w - core + c
        for ts in seq_to:
            remote(s3n.at[c, ts], r3n.at[slot3], 3, (ts, tw)).start()
            remote(s3t.at[c], r3t.at[slot3], 4, (ts, tw)).start()

        @pl.when(core != c)
        def _():
            remote(s3n.at[c, s], r3n.at[slot3], 3, (s, tw)).start()
            remote(s3t.at[c], r3t.at[slot3], 4, (s, tw)).start()

        @pl.when(core == c)
        def _():
            r3n[slot3] = s3n[c, s]
            r3t[slot3] = s3t[c]

    @pl.when(w < 2)
    def _():
        parts = []
        for i in range(4):
            b = core * 4 + i
            qrow = qt[b, pl.ds(s * GROUP, GROUP), :]
            sn = jnp.sum(qrow * knew[pl.ds(b, 1), :], axis=-1, keepdims=True) * scale
            parts.append(jnp.broadcast_to(sn, (GROUP, HD)))
        r3t[16] = jnp.where(low16, by_block(parts), 1.0)
        r3n[16] = jnp.concatenate(
            [jnp.broadcast_to(vnew[pl.ds(core * 4 + i, 1), :], (GROUP, HD)) for i in range(4)], axis=0
        ).astype(bf16)

    @pl.when(w >= 2)
    def _():
        r3t[16] = jnp.where(low16, neg_large, 0.0)
        r3n[16] = jnp.zeros((32, HD), bf16)

    remote(r3t.at[pl.ds(0, 15)], r3t.at[pl.ds(0, 15)], 4, (s, w)).wait_recv()
    remote(r3n.at[pl.ds(0, 15)], r3n.at[pl.ds(0, 15)], 3, (s, w)).wait_recv()

    def merge(stats, numers):
        peak = stats[0]
        for t in stats[1:]:
            peak = jnp.maximum(peak, t)
        total = jnp.zeros((GROUP, HD), f32)
        acc = [jnp.zeros((GROUP, HD), f32) for _ in range(4)]
        for t, n in zip(stats, numers):
            f = jnp.exp(t - peak)
            total = total + f * pltpu.roll(t, HD - 16, 1)
            for i in range(4):
                acc[i] = acc[i] + jnp.broadcast_to(f[:, 32 * i : 32 * i + 1], (GROUP, HD)) * n[
                    i * GROUP : (i + 1) * GROUP
                ]
        return peak, total, acc

    shift = (HD - s) % HD
    peak, total, acc = merge(
        [pltpu.roll(r3t[i], shift, 1) for i in range(17)],
        [r3n[i].astype(f32) for i in range(17)],
    )
    s4t[...] = jnp.where(low16, peak, pltpu.roll(total, 16, 1))
    s4n[...] = jnp.concatenate(acc, axis=0).astype(bf16)
    for tw in wide_to:
        remote(s4n, r4n.at[w], 5, (s, tw)).start()
        remote(s4t, r4t.at[w], 6, (s, tw)).start()
    r4n[w] = s4n[...]
    r4t[w] = s4t[...]
    small[7].wait()
    remote(r4t.at[pl.ds(0, 15)], r4t.at[pl.ds(0, 15)], 6, (s, w)).wait_recv()
    remote(r4n.at[pl.ds(0, 15)], r4n.at[pl.ds(0, 15)], 5, (s, w)).wait_recv()
    for c in range(2):
        peak, total, acc = merge(
            [r4t[2 * i + c] for i in range(8)], [r4n[2 * i + c].astype(f32) for i in range(8)]
        )
        for i in range(4):
            den = jnp.broadcast_to(total[:, 32 * i : 32 * i + 1], (GROUP, HD))
            of[pl.ds((c * 4 + i) * GROUP, GROUP), :] = acc[i] / den

    o = jnp.concatenate(
        [of[pl.ds(j, ROWS, stride=GROUP), :].astype(bf16) for j in range(GROUP)], axis=1
    )
    s5[...] = lax.dot_general(o, wo_v[...], (((1,), (1,)), ((), ())), preferred_element_type=f32)
    for ts in seq_to:
        remote(s5, r5.at[s], 7, (ts, w)).start()
    r5[s] = s5[...]
    remote(r5.at[pl.ds(0, 7)], r5.at[pl.ds(0, 7)], 7, (s, w)).wait_recv()
    out = r5[0]
    for i in range(1, NSEQ):
        out = out + r5[i]
    out_ref[...] = out

    remote(r1.at[pl.ds(0, 15)], r1.at[pl.ds(0, 15)], 0, (s, w)).wait_send()
    for t in range(2):

        @pl.when(w != t)
        def _():
            remote(skv, rkv.at[w], 1, (s, t)).wait_send()

    remote(qall.at[pl.ds(0, 31)], qall.at[pl.ds(0, 31)], 2, (s, w)).wait_send()
    remote(r3n.at[pl.ds(0, 15)], r3n.at[pl.ds(0, 15)], 3, (s, w)).wait_send()
    remote(r3t.at[pl.ds(0, 15)], r3t.at[pl.ds(0, 15)], 4, (s, w)).wait_send()
    remote(r4n.at[pl.ds(0, 15)], r4n.at[pl.ds(0, 15)], 5, (s, w)).wait_send()
    remote(r4t.at[pl.ds(0, 15)], r4t.at[pl.ds(0, 15)], 6, (s, w)).wait_send()
    remote(r5.at[pl.ds(0, 7)], r5.at[pl.ds(0, 7)], 7, (s, w)).wait_send()


def body(
    activations, attn_gain, w_query, w_keyval, w_output, query_gain, key_gain, key_cache, value_cache, lengths
):
    half = HD // 2
    freq = np.exp(-(2.0 * np.arange(half) / HD) * math.log(rope_base)).astype(np.float32)
    freq = jnp.asarray(np.concatenate([freq, freq])[None, :])
    any_spec = pl.BlockSpec(memory_space=pl.ANY)
    vm = pltpu.VMEM
    return pl.pallas_call(
        kernel,
        out_shape=jax.ShapeDtypeStruct((ROWS, WIDTH), f32),
        in_specs=[any_spec] * 10 + [pl.BlockSpec(memory_space=pltpu.SMEM)],
        out_specs=pl.BlockSpec(memory_space=pltpu.VMEM),
        scratch_shapes=[
            vm((ROWS, WIDTH), bf16),
            vm((WIDTH,), f32),
            vm((WIDTH, 1024), bf16),
            vm((2 * WIDTH, HD), bf16),
            vm((WIDTH, 1024), bf16),
            vm((1, HD), f32),
            vm((1, HD), f32),
            vm((ROWS, FLAT, HD), bf16),
            vm((ROWS, FLAT, HD), bf16),
            vm((1, HD), f32),
            vm((4, 3, ROWS, HD), f32),
            vm((NWIDE, 3, ROWS, HD), f32),
            vm((2, ROWS, HD), f32),
            vm((NWIDE, 2, ROWS, HD), f32),
            vm((16, HD), bf16),
            vm((32, 16, HD), bf16),
            vm((HEADS * ROWS, HD), f32),
            vm((ROWS, HEADS, HD), f32),
            vm((ROWS, HD), f32),
            vm((ROWS, HD), f32),
            vm((CHUNKS, GROUP, CHUNK), f32),
            vm((ROWS, GROUP, HD), f32),
            vm((ROWS, GROUP, HD), f32),
            vm((ROWS, KVH, GROUP, HD), f32),
            vm((2, KVH, 32, HD), bf16),
            vm((2, GROUP, HD), f32),
            vm((17, 32, HD), bf16),
            vm((17, GROUP, HD), f32),
            vm((32, HD), bf16),
            vm((GROUP, HD), f32),
            vm((NWIDE, 32, HD), bf16),
            vm((NWIDE, GROUP, HD), f32),
            vm((HEADS, HD), f32),
            vm((ROWS, WIDTH), f32),
            vm((NSEQ, ROWS, WIDTH), f32),
            pltpu.SemaphoreType.DMA((8,)),
            pltpu.SemaphoreType.DMA((ROWS,)),
            pltpu.SemaphoreType.DMA((ROWS,)),
            pltpu.SemaphoreType.DMA((8,)),
            pltpu.SemaphoreType.DMA((8,)),
        ],
        compiler_params=pltpu.CompilerParams(
            collective_id=0, has_side_effects=True, vmem_limit_bytes=60 * 1024 * 1024
        ),
    )(
        activations,
        attn_gain,
        w_query,
        w_keyval.reshape(2 * WIDTH, HD),
        w_output.T,
        query_gain.reshape(1, HD),
        key_gain.reshape(1, HD),
        key_cache.reshape(ROWS, FLAT, HD),
        value_cache.reshape(ROWS, FLAT, HD),
        freq,
        lengths,
    )


def solution(mesh):
    return jax.shard_map(
        body,
        mesh=mesh,
        in_specs=(
            P(None, "wide"),
            P("wide"),
            P("wide", "seq"),
            P("wide", None, "seq"),
            P("seq", "wide"),
            P(),
            P(),
            P(None, ("seq", "wide"), None, None),
            P(None, ("seq", "wide"), None, None),
            P(),
        ),
        out_specs=P(None, "wide"),
        check_vma=False,
    )
```

time: 854 us -> 43 us (0.05); the launches traced: 841 us -> 42.8 us
  blocking collectives: 546 us -> 0 us
  other arithmetic: 263 us -> 0 us
  Pallas kernels: 0 us -> 41.5 us
  between operations: 13.5 us -> 0.01 us
  matrix products: 10.6 us -> 0 us
    all_gather x5 -> x0, blocking collectives: 445 us -> none  [the longest x2 369 us: joined(): everything = jax.tree.map(lambda part: lax.all_gather(part, axis), shard)]
    add x255 -> x0, other arithmetic: 258 us -> none  [the longest x127 154 us: combine(): numer_a * factor_a[..., None] + numer_b * factor_b[..., None]]
    psum x2 -> x0, blocking collectives: 100 us -> none  [the longest x1 69.8 us: body(): lax.psum((square_sum, part_query, part_keyval), 'wide')]
    pallas_call x0 -> x1, Pallas kernels: none -> 41.5 us  [body(): pl.pallas_call(kernel, out_shape=jax.ShapeDtypeStruct((ROWS, WIDTH), f32)...]
    dot_general x6 -> x0, matrix products: 10.6 us -> none  [the longest x1 5.76 us: body(): jnp.einsum('bgjd,btgd->bgjt', grouped, key_cache, preferred_element_type=...]
  transfers between devices with their start and end apart: 1 -> 0, of which waited for: 0 -> 0; matrix products, arithmetic and copies ran while one was open for 0% -> 0% of each run, Pallas kernels for 0% -> 0%
where the time goes in v1:
time: 43 us; the launch traced here: 42.8 us
  Pallas kernels  41.5 us (97%)
  local copies, waits for them, and re-layouts  1.31 us (3%)
    pallas_call x1, Pallas kernels, body(): pl.pallas_call(kernel, out_shape=jax.ShapeDtypeStruct((ROWS, WIDTH), f32)...  41.5 us
    unnamed x1, local copies, waits for them, and re-layouts  1.31 us

profile of v1, /device:TPU:0, one launch (start us, length us, event | category | flops | bytes accessed | tf_op | source)
XLA Modules:
  0.0 42.8 jit_solution(9581695263811390143)
XLA Ops:
  0.0 41.5 %shard_map.109 = f32[8,320]{1,0:T(8,128)} custom-call(bf16[8,320]{1,0:T(8,128)(2,1)} %x_hbm.1, f32[320]{0:T(512)} %gain_hbm.1, bf16[320,1024]{1,0:T(8,128)(2,1)} %wq_hbm.1, bf16[640,128]{1,0:T(8,128)(2,1)} %bitcast.9, bf16[320,1024]{1,0:T(8,128)(2,1)} %bitcast.8, f32[1,128]{1,0:T(1,128)} %bitcast.10, f32[1,128]{1,0:T(1,128)} %bitcast.11, ...), custom_call_target="tpu_custom_call" | custom-call | tf_op jit(solution)/shard_map/pallas_call | solution.py:375
  41.5 1.3 %copy.13 = f32[8,320]{1,0:T(8,128)} copy(f32[8,320]{1,0:T(8,128)} %shard_map.109) | data formatting | bytes 20480

commit v2 on v1

--- a/solution.py
+++ b/solution.py
@@ -19,8 +19,6 @@
 HEADS = KVH * GROUP
 BLOCK = 512
 FLAT = BLOCK * KVH
-CHUNK = 512
-CHUNKS = FLAT // CHUNK
 NSEQ, NWIDE = 8, 16
 WIDTH = 320
 D = 5120
@@ -34,7 +32,7 @@
     x_hbm, gain_hbm, wq_hbm, wkv_hbm, wo_hbm, qg_hbm, kg_hbm, k_hbm, v_hbm, freq_hbm, len_ref,
     out_ref,
     x_v, gain_v, wq_v, wkv_v, wo_v, qg_v, kg_v, k_v, v_v, freq_v,
-    s1, r1, skv, rkv, sq, qall, qf, qt, knew, vnew, scr, mst, lst, numf,
+    k_t, v_r, s1, r1, skv, rkv, sq, qall, qf, qt, knew, vnew, scr, pb,
     s3n, s3t, r3n, r3t, s4n, s4t, r4n, r4t, of, s5, r5,
     in_sem, k_sem, v_sem, ssem, rsem,
 ):
@@ -117,12 +115,29 @@
     xf = x_v[...].astype(f32)
     ss = jnp.sum(xf * xf, axis=-1, keepdims=True)
     normed = (xf * gain_v[...][None, :]).astype(bf16)
+    row = lax.broadcasted_iota(jnp.int32, (ROWS, HD), 0)
+    lane = lane_iota((ROWS, HD))
+    ss_row = jnp.sum(jnp.where(lane == row, ss, 0.0), axis=0, keepdims=True)
     for p in range(4):
         part = jnp.dot(normed, wq_v[:, p * 256 : (p + 1) * 256], preferred_element_type=f32)
-        s1[p, 0] = part[:, :HD]
-        s1[p, 1] = part[:, HD:]
-        s1[p, 2] = jnp.broadcast_to(ss, (ROWS, HD))
+        s1[p, 0:ROWS] = part[:, :HD]
+        s1[p, ROWS : 2 * ROWS] = part[:, HD:]
+        s1[p, 2 * ROWS : 2 * ROWS + 1] = ss_row
     r1[w] = s1[w % 4]
+
+    def turn_k(b, carry):
+        pltpu.make_async_copy(k_hbm.at[b], k_v.at[b], k_sem.at[b]).wait()
+        for ch in range(2):
+            part = k_v[b, pl.ds(ch * 2048, 2048), :].reshape(256, KVH, HD).reshape(256, KVH * HD)
+            k_t[b, :, ch * 256 : (ch + 1) * 256] = part.T
+        return carry
+
+    def turn_v(b, carry):
+        pltpu.make_async_copy(v_hbm.at[b], v_v.at[b], v_sem.at[b]).wait()
+        for ch in range(2):
+            part = v_v[b, pl.ds(ch * 2048, 2048), :].reshape(256, KVH, HD)
+            v_r[b, pl.ds(ch * 256, 256), :] = part.reshape(256, KVH * HD)
+        return carry
 
     pl.semaphore_wait(bar, n_bar)
     for tw in wide_to:
@@ -140,18 +155,7 @@
     kv_part = jnp.dot(both, wkv_v[...], preferred_element_type=f32)
     skv[0] = kv_part[:ROWS]
     skv[1] = kv_part[ROWS:]
-    for t in range(2):
-
-        @pl.when(w != t)
-        def _():
-            remote(skv, rkv.at[w], 1, (s, t)).start()
-
-        @pl.when(w == t)
-        def _():
-            rkv[w] = skv[...]
-
-    row = lax.broadcasted_iota(jnp.int32, (ROWS, HD), 0)
-    lane = lane_iota((ROWS, HD))
+
     lens = jnp.zeros((ROWS, HD), jnp.int32)
     for b in range(ROWS):
         lens = jnp.where(row == b, len_ref[b], lens)
@@ -163,13 +167,28 @@
         u = u * lax.rsqrt(jnp.mean(u * u, axis=-1, keepdims=True) + eps_norm) * gain
         return u * cosine + pltpu.roll(u, HD // 2, 1) * sine
 
+    for t in range(2):
+
+        @pl.when(w != t)
+        def _():
+            remote(skv, rkv.at[w], 1, (s, t)).start()
+
+        @pl.when(w == t)
+        def _():
+            rkv[w] = skv[...]
+
+    lax.fori_loop(0, 4, turn_k, 0)
+
     remote(r1.at[pl.ds(0, NWIDE - 1)], r1.at[pl.ds(0, NWIDE - 1)], 0, (s, w)).wait_recv()
     tot = r1[0]
     for i in range(1, NWIDE):
         tot = tot + r1[i]
-    inv_rms = lax.rsqrt(tot[2] / D + eps_norm)
+    ss = jnp.sum(
+        jnp.where(lane == row, tot[2 * ROWS : 2 * ROWS + 1], 0.0), axis=-1, keepdims=True
+    )
+    inv_rms = lax.rsqrt(ss / D + eps_norm)
     sq[...] = jnp.concatenate(
-        [head(tot[0] * inv_rms, qg_v[...]), head(tot[1] * inv_rms, qg_v[...])], axis=0
+        [head(tot[:ROWS] * inv_rms, qg_v[...]), head(tot[ROWS : 2 * ROWS] * inv_rms, qg_v[...])], axis=0
     ).astype(bf16)
 
     p_own = w % 4
@@ -186,6 +205,9 @@
         knew[...] = head(kv[0] * inv_rms, kg_v[...]).astype(bf16).astype(f32)
         vnew[...] = (kv[1] * inv_rms).astype(bf16).astype(f32)
 
+    lax.fori_loop(4, ROWS, turn_k, 0)
+    lax.fori_loop(0, ROWS, turn_v, 0)
+
     remote(qall.at[pl.ds(0, 31)], qall.at[pl.ds(0, 31)], 2, (s, w)).wait_recv()
     qf[...] = qall[...].reshape(HEADS * ROWS, HD).astype(f32)
     for b in range(ROWS):
@@ -193,89 +215,71 @@
 
     scale = HD ** (-0.5)
     start = (s * NWIDE + w) * BLOCK
-    clane = lane_iota((GROUP, CHUNK))
-    bit0 = clane % 2 == 1
-    bit1 = (clane // 2) % 2 == 1
-    bit2 = (clane // 4) % 2 == 1
-    of_group = [clane % KVH == g for g in range(KVH)]
-
-    def attend(b, carry):
-        q = qt[b].astype(bf16)
-        limit = (len_ref[b] - start) * KVH
-        peak = jnp.full((GROUP, CHUNK), neg_large, f32)
-        for ch in range(CHUNKS):
-            keys = k_v[b, pl.ds(ch * CHUNK, CHUNK), :]
-            sc = lax.dot_general(q, keys, (((1,), (1,)), ((), ())), preferred_element_type=f32)
-            g = [sc[i * GROUP : (i + 1) * GROUP] for i in range(KVH)]
-            g = [jnp.where(bit0, g[i + 1], g[i]) for i in range(0, 8, 2)]
-            g = [jnp.where(bit1, g[i + 1], g[i]) for i in range(0, 4, 2)]
-            t = jnp.where(bit2, g[1], g[0]) * scale
-            t = jnp.where(clane + ch * CHUNK < limit, t, neg_large)
-            scr[ch] = t
-            peak = jnp.maximum(peak, t)
-        m = jnp.maximum(
-            jnp.maximum(peak[:, 0:128], peak[:, 128:256]),
-            jnp.maximum(peak[:, 256:384], peak[:, 384:512]),
-        )
-        for sh in (64, 32, 16, 8):
-            m = jnp.maximum(m, pltpu.roll(m, sh, 1))
-        m4 = jnp.concatenate([m, m, m, m], axis=1)
-        total = jnp.zeros((GROUP, CHUNK), f32)
-        num = jnp.zeros((HEADS, HD), f32)
-        for ch in range(CHUNKS):
-            e = jnp.exp(scr[ch] - m4)
-            e = jnp.where(clane + ch * CHUNK < limit, e, 0.0)
-            total = total + e
-            wide_e = jnp.concatenate(
-                [jnp.where(of_group[g], e, 0.0) for g in range(KVH)], axis=0
-            ).astype(bf16)
-            num = num + jnp.dot(
-                wide_e, v_v[b, pl.ds(ch * CHUNK, CHUNK), :], preferred_element_type=f32
-            )
-        tl = total[:, 0:128] + total[:, 128:256] + total[:, 256:384] + total[:, 384:512]
-        for sh in (64, 32, 16, 8):
-            tl = tl + pltpu.roll(tl, sh, 1)
-        mst[b] = m
-        lst[b] = tl
-        numf[b] = num.reshape(KVH, GROUP, HD)
-        return carry
-
-    block32 = lane // 32
+    plane = lane_iota((HEADS, BLOCK))
+    none = jnp.zeros((GROUP, HD), f32)
+    block32 = lane_iota((HEADS, HD)) // 32
+    low = lane_iota((HEADS, HD)) % 32 < 16
     low16 = lane % 32 < 16
 
     def by_block(parts):
+        n = parts[0].shape[0]
         out = parts[0]
         for i in range(1, 4):
-            out = jnp.where(block32 == i, parts[i], out)
+            out = jnp.where(block32[:n] == i, parts[i], out)
         return out
 
     slot3 = s * 2 + core
     for c in range(2):
-        for b in range(c * 4, c * 4 + 4):
-            k_cp[b].wait()
-            v_cp[b].wait()
-        lax.fori_loop(c * 4, c * 4 + 4, attend, 0)
+        rows = range(c * 4, c * 4 + 4)
+        scores, peaks, totals, weights, numers = {}, {}, {}, {}, {}
+        for b in rows:
+            parts = []
+            for pr in range(4):
+                one = qt[b, 16 * pr : 16 * pr + 8, :]
+                two = qt[b, 16 * pr + 8 : 16 * pr + 16, :]
+                lhs = jnp.concatenate(
+                    [jnp.concatenate([one, none], axis=1), jnp.concatenate([none, two], axis=1)],
+                    axis=0,
+                ).astype(bf16)
+                keys = k_t[b, pr * 256 : (pr + 1) * 256, :]
+                parts.append(jnp.dot(lhs, keys, preferred_element_type=f32))
+            scr[b % 4] = jnp.concatenate(parts, axis=0)
+        for b in rows:
+            valid = plane < len_ref[b] - start
+            t = jnp.where(valid, scr[b % 4] * scale, neg_large)
+            m = jnp.max(t, axis=-1, keepdims=True)
+            e = jnp.where(valid, jnp.exp(t - m), 0.0)
+            peaks[b] = jnp.broadcast_to(m, (HEADS, HD))
+            totals[b] = jnp.broadcast_to(jnp.sum(e, axis=-1, keepdims=True), (HEADS, HD))
+            pb[b % 4] = e.astype(bf16)
+        for b in rows:
+            for pr in range(4):
+                n = jnp.dot(
+                    pb[b % 4, 16 * pr : 16 * pr + 16, :],
+                    v_r[b, :, pr * 256 : (pr + 1) * 256],
+                    preferred_element_type=f32,
+                )
+                numers[b, 2 * pr] = n[:GROUP, :HD]
+                numers[b, 2 * pr + 1] = n[GROUP:, HD:]
         s3t[c] = jnp.where(
-            low16,
-            by_block([mst[c * 4 + i] for i in range(4)]),
-            by_block([lst[c * 4 + i] for i in range(4)]),
-        )
+            low, by_block([peaks[b] for b in rows]), by_block([totals[b] for b in rows])
+        ).reshape(KVH, GROUP, HD)
         for g in range(KVH):
-            s3n[c, g] = jnp.concatenate([numf[c * 4 + i, g] for i in range(4)], axis=0).astype(bf16)
+            s3n[c, g] = jnp.concatenate([numers[b, g] for b in rows], axis=0).astype(bf16)
         tw = w - core + c
         for ts in seq_to:
             remote(s3n.at[c, ts], r3n.at[slot3], 3, (ts, tw)).start()
-            remote(s3t.at[c], r3t.at[slot3], 4, (ts, tw)).start()
+            remote(s3t.at[c, ts], r3t.at[slot3], 4, (ts, tw)).start()
 
         @pl.when(core != c)
         def _():
             remote(s3n.at[c, s], r3n.at[slot3], 3, (s, tw)).start()
-            remote(s3t.at[c], r3t.at[slot3], 4, (s, tw)).start()
+            remote(s3t.at[c, s], r3t.at[slot3], 4, (s, tw)).start()
 
         @pl.when(core == c)
         def _():
             r3n[slot3] = s3n[c, s]
-            r3t[slot3] = s3t[c]
+            r3t[slot3] = s3t[c, s]
 
     @pl.when(w < 2)
     def _():
@@ -313,9 +317,8 @@
                 ]
         return peak, total, acc
 
-    shift = (HD - s) % HD
     peak, total, acc = merge(
-        [pltpu.roll(r3t[i], shift, 1) for i in range(17)],
+        [r3t[i] for i in range(17)],
         [r3n[i].astype(f32) for i in range(17)],
     )
     s4t[...] = jnp.where(low16, peak, pltpu.roll(total, 16, 1))
@@ -374,7 +377,7 @@
     vm = pltpu.VMEM
     return pl.pallas_call(
         kernel,
-        out_shape=jax.ShapeDtypeStruct((ROWS, WIDTH), f32),
+        out_shape=pltpu.VMEM((ROWS, WIDTH), f32),
         in_specs=[any_spec] * 10 + [pl.BlockSpec(memory_space=pltpu.SMEM)],
         out_specs=pl.BlockSpec(memory_space=pltpu.VMEM),
         scratch_shapes=[
@@ -388,8 +391,10 @@
             vm((ROWS, FLAT, HD), bf16),
             vm((ROWS, FLAT, HD), bf16),
             vm((1, HD), f32),
-            vm((4, 3, ROWS, HD), f32),
-            vm((NWIDE, 3, ROWS, HD), f32),
+            vm((ROWS, KVH * HD, BLOCK), bf16),
+            vm((ROWS, BLOCK, KVH * HD), bf16),
+            vm((4, 17, HD), f32),
+            vm((NWIDE, 17, HD), f32),
             vm((2, ROWS, HD), f32),
             vm((NWIDE, 2, ROWS, HD), f32),
             vm((16, HD), bf16),
@@ -398,12 +403,10 @@
             vm((ROWS, HEADS, HD), f32),
             vm((ROWS, HD), f32),
             vm((ROWS, HD), f32),
-            vm((CHUNKS, GROUP, CHUNK), f32),
-            vm((ROWS, GROUP, HD), f32),
-            vm((ROWS, GROUP, HD), f32),
-            vm((ROWS, KVH, GROUP, HD), f32),
+            vm((4, HEADS, BLOCK), f32),
+            vm((4, HEADS, BLOCK), bf16),
             vm((2, KVH, 32, HD), bf16),
-            vm((2, GROUP, HD), f32),
+            vm((2, KVH, GROUP, HD), f32),
             vm((17, 32, HD), bf16),
             vm((17, GROUP, HD), f32),
             vm((32, HD), bf16),

time: 43 us -> 35.5 us (0.83)
  Pallas kernels: 41.5 us -> 34.5 us
  local copies, waits for them, and re-layouts: 1.31 us -> 0.6 us
    pallas_call x1, Pallas kernels: 41.5 us -> 34.5 us  [body(): pl.pallas_call(kernel, out_shape=pltpu.VMEM((ROWS, WIDTH), f32), in_specs...]
    unnamed x1, local copies, waits for them, and re-layouts: 1.31 us -> 0.6 us
where the time goes in v2:
time: 35.5 us; the launch traced here: 35.1 us
  Pallas kernels  34.5 us (97%)
  local copies, waits for them, and re-layouts  0.6 us (2%)
    pallas_call x1, Pallas kernels, body(): pl.pallas_call(kernel, out_shape=pltpu.VMEM((ROWS, WIDTH), f32), in_specs...  34.5 us

profile of v2, /device:TPU:0, one launch (start us, length us, event | category | flops | bytes accessed | tf_op | source)
XLA Modules:
  0.0 35.1 jit_solution(10256026983744232136)
XLA Ops:
  0.0 34.5 %shard_map.109 = f32[8,320]{1,0:T(8,128)S(1)} custom-call(bf16[8,320]{1,0:T(8,128)(2,1)} %x_hbm.1, f32[320]{0:T(512)} %gain_hbm.1, bf16[320,1024]{1,0:T(8,128)(2,1)} %wq_hbm.1, bf16[640,128]{1,0:T(8,128)(2,1)} %bitcast.9, bf16[320,1024]{1,0:T(8,128)(2,1)} %bitcast.8, f32[1,128]{1,0:T(1,128)} %bitcast.10, f32[1,128]{1,0:T(1,128)} %bitcast.11, ...), custom_call_target="tpu_custom_call" | custom-call | tf_op jit(solution)/shard_map/pallas_call | solution.py:378
  34.5 0.6 %copy.13 = f32[8,320]{1,0:T(8,128)} copy(f32[8,320]{1,0:T(8,128)S(1)} %shard_map.109) | data formatting | bytes 20480

commit v3 on v2

--- a/solution.py
+++ b/solution.py
@@ -33,7 +33,7 @@
     out_ref,
     x_v, gain_v, wq_v, wkv_v, wo_v, qg_v, kg_v, k_v, v_v, freq_v,
     k_t, v_r, s1, r1, skv, rkv, sq, qall, qf, qt, knew, vnew, scr, pb,
-    s3n, s3t, r3n, r3t, s4n, s4t, r4n, r4t, of, s5, r5,
+    s3, r3, s4, r4, of, s5, r5,
     in_sem, k_sem, v_sem, ssem, rsem,
 ):
     s = lax.axis_index("seq")
@@ -62,30 +62,39 @@
     for c in small[:6]:
         c.start()
 
-    wide_to = []
-    for kx in (2, 1, 3, 0):
-        for ky in (1, 0):
-            for kc in (0, 1):
-                if kx or ky or kc:
-                    wide_to.append(((x + kx) % 4) * 4 + ((yh + ky) % 2) * 2 + (core + kc) % 2)
-    plane_to = []
-    for kz in (2, 1, 3, 0):
-        for ky in (1, 0):
-            for kh in (1, 0):
-                for kc in (0, 1):
-                    if kz or ky or kh or kc:
-                        plane_to.append(
-                            (
-                                ((yl + ky) % 2) * 4 + (z + kz) % 4,
-                                x * 4 + ((yh + kh) % 2) * 2 + (core + kc) % 2,
-                                bool(kz or ky),
-                            )
-                        )
-    seq_to = []
-    for kz in (2, 1, 3, 0):
-        for ky in (1, 0):
-            if kz or ky:
-                seq_to.append(((yl + ky) % 2) * 4 + (z + kz) % 4)
+    def ring(k):
+        return min(k, 4 - k)
+
+    def y_hops(hi, lo):
+        return 1 if lo else 2 * hi
+
+    steps = [(kx, hi, kc) for kx in range(4) for hi in range(2) for kc in range(2)]
+    steps.sort(key=lambda k: (-ring(k[0]) - y_hops(k[1], 0), -k[2]))
+    wide_to = [
+        ((x + kx) % 4) * 4 + ((yh + hi) % 2) * 2 + (core + kc) % 2
+        for kx, hi, kc in steps
+        if kx or hi or kc
+    ]
+    steps = [
+        (kz, hi, lo, kc)
+        for kz in range(4)
+        for hi in range(2)
+        for lo in range(2)
+        for kc in range(2)
+    ]
+    steps.sort(key=lambda k: (-ring(k[0]) - y_hops(k[1], k[2]), -k[3]))
+    plane_to = [
+        (
+            ((yl + lo) % 2) * 4 + (z + kz) % 4,
+            x * 4 + ((yh + hi) % 2) * 2 + (core + kc) % 2,
+            bool(kz or lo),
+        )
+        for kz, hi, lo, kc in steps
+        if kz or hi or lo or kc
+    ]
+    steps = [(kz, lo) for kz in range(4) for lo in range(2)]
+    steps.sort(key=lambda k: -ring(k[0]) - k[1])
+    seq_to = [((yl + lo) % 2) * 4 + (z + kz) % 4 for kz, lo in steps if kz or lo]
 
     bar = pltpu.get_barrier_semaphore()
     n_bar = 0
@@ -97,18 +106,18 @@
             pl.semaphore_signal(bar, inc=1, device_id=(ts, tw), device_id_type=MESH)
             n_bar += 1
 
+    def remote(src, dst, i, to):
+        return pltpu.make_async_remote_copy(
+            src_ref=src, dst_ref=dst, send_sem=ssem.at[i], recv_sem=rsem.at[i],
+            device_id=to, device_id_type=MESH,
+        )
+
     for c in small[6:]:
         c.start()
     k_cp = [pltpu.make_async_copy(k_hbm.at[b], k_v.at[b], k_sem.at[b]) for b in range(ROWS)]
     v_cp = [pltpu.make_async_copy(v_hbm.at[b], v_v.at[b], v_sem.at[b]) for b in range(ROWS)]
     for c in k_cp + v_cp:
         c.start()
-
-    def remote(src, dst, i, to):
-        return pltpu.make_async_remote_copy(
-            src_ref=src, dst_ref=dst, send_sem=ssem.at[i], recv_sem=rsem.at[i],
-            device_id=to, device_id_type=MESH,
-        )
 
     for c in small[:6]:
         c.wait()
@@ -163,8 +172,9 @@
     cosine = jnp.cos(angle)
     sine = jnp.where(lane < HD // 2, -jnp.sin(angle), jnp.sin(angle))
 
-    def head(u, gain):
-        u = u * lax.rsqrt(jnp.mean(u * u, axis=-1, keepdims=True) + eps_norm) * gain
+    def head(u, inv_rms, gain):
+        mean = jnp.mean(u * u, axis=-1, keepdims=True) * (inv_rms * inv_rms)
+        u = u * gain * (inv_rms * lax.rsqrt(mean + eps_norm))
         return u * cosine + pltpu.roll(u, HD // 2, 1) * sine
 
     for t in range(2):
@@ -188,22 +198,14 @@
     )
     inv_rms = lax.rsqrt(ss / D + eps_norm)
     sq[...] = jnp.concatenate(
-        [head(tot[:ROWS] * inv_rms, qg_v[...]), head(tot[ROWS : 2 * ROWS] * inv_rms, qg_v[...])], axis=0
+        [head(tot[:ROWS], inv_rms, qg_v[...]), head(tot[ROWS : 2 * ROWS], inv_rms, qg_v[...])],
+        axis=0,
     ).astype(bf16)
 
     p_own = w % 4
     for ts, tw, _far in plane_to:
         remote(sq, qall.at[s * 4 + p_own], 2, (ts, tw)).start()
     qall[s * 4 + p_own] = sq[...]
-
-    @pl.when(w < 2)
-    def _():
-        remote(rkv.at[pl.ds(0, NWIDE - 1)], rkv.at[pl.ds(0, NWIDE - 1)], 1, (s, w)).wait_recv()
-        kv = rkv[0]
-        for i in range(1, NWIDE):
-            kv = kv + rkv[i]
-        knew[...] = head(kv[0] * inv_rms, kg_v[...]).astype(bf16).astype(f32)
-        vnew[...] = (kv[1] * inv_rms).astype(bf16).astype(f32)
 
     lax.fori_loop(4, ROWS, turn_k, 0)
     lax.fori_loop(0, ROWS, turn_v, 0)
@@ -227,6 +229,11 @@
         for i in range(1, 4):
             out = jnp.where(block32[:n] == i, parts[i], out)
         return out
+
+    def pack(peak, total):
+        high = total.astype(bf16).astype(f32)
+        n = low[: peak.shape[0]]
+        return jnp.where(n, peak, high), jnp.where(n, 0.0, total - high)
 
     slot3 = s * 2 + core
     for c in range(2):
@@ -247,7 +254,7 @@
         for b in rows:
             valid = plane < len_ref[b] - start
             t = jnp.where(valid, scr[b % 4] * scale, neg_large)
-            m = jnp.max(t, axis=-1, keepdims=True)
+            m = jnp.max(t, axis=-1, keepdims=True).astype(bf16).astype(f32)
             e = jnp.where(valid, jnp.exp(t - m), 0.0)
             peaks[b] = jnp.broadcast_to(m, (HEADS, HD))
             totals[b] = jnp.broadcast_to(jnp.sum(e, axis=-1, keepdims=True), (HEADS, HD))
@@ -261,80 +268,86 @@
                 )
                 numers[b, 2 * pr] = n[:GROUP, :HD]
                 numers[b, 2 * pr + 1] = n[GROUP:, HD:]
-        s3t[c] = jnp.where(
-            low, by_block([peaks[b] for b in rows]), by_block([totals[b] for b in rows])
-        ).reshape(KVH, GROUP, HD)
+        stats = pack(by_block([peaks[b] for b in rows]), by_block([totals[b] for b in rows]))
         for g in range(KVH):
-            s3n[c, g] = jnp.concatenate([numers[b, g] for b in rows], axis=0).astype(bf16)
+            own = slice(g * GROUP, (g + 1) * GROUP)
+            s3[c, g] = jnp.concatenate(
+                [numers[b, g] for b in rows] + [part[own] for part in stats], axis=0
+            ).astype(bf16)
         tw = w - core + c
         for ts in seq_to:
-            remote(s3n.at[c, ts], r3n.at[slot3], 3, (ts, tw)).start()
-            remote(s3t.at[c, ts], r3t.at[slot3], 4, (ts, tw)).start()
+            remote(s3.at[c, ts], r3.at[slot3], 3, (ts, tw)).start()
 
         @pl.when(core != c)
         def _():
-            remote(s3n.at[c, s], r3n.at[slot3], 3, (s, tw)).start()
-            remote(s3t.at[c, s], r3t.at[slot3], 4, (s, tw)).start()
+            remote(s3.at[c, s], r3.at[slot3], 3, (s, tw)).start()
 
         @pl.when(core == c)
         def _():
-            r3n[slot3] = s3n[c, s]
-            r3t[slot3] = s3t[c, s]
+            r3[slot3] = s3[c, s]
 
     @pl.when(w < 2)
     def _():
-        parts = []
+        remote(rkv.at[pl.ds(0, NWIDE - 1)], rkv.at[pl.ds(0, NWIDE - 1)], 1, (s, w)).wait_recv()
+        kv = rkv[0]
+        for i in range(1, NWIDE):
+            kv = kv + rkv[i]
+        knew[...] = head(kv[0], inv_rms, kg_v[...]).astype(bf16).astype(f32)
+        vnew[...] = (kv[1] * inv_rms).astype(bf16).astype(f32)
+
+    @pl.when(w < 2)
+    def _():
+        peaks, totals, numers = [], [], []
         for i in range(4):
             b = core * 4 + i
             qrow = qt[b, pl.ds(s * GROUP, GROUP), :]
             sn = jnp.sum(qrow * knew[pl.ds(b, 1), :], axis=-1, keepdims=True) * scale
-            parts.append(jnp.broadcast_to(sn, (GROUP, HD)))
-        r3t[16] = jnp.where(low16, by_block(parts), 1.0)
-        r3n[16] = jnp.concatenate(
-            [jnp.broadcast_to(vnew[pl.ds(core * 4 + i, 1), :], (GROUP, HD)) for i in range(4)], axis=0
+            sn = jnp.broadcast_to(sn, (GROUP, HD))
+            mn = sn.astype(bf16).astype(f32)
+            pn = jnp.exp(sn - mn)
+            peaks.append(mn)
+            totals.append(pn)
+            numers.append(pn.astype(bf16).astype(f32) * vnew[pl.ds(b, 1), :])
+        r3[16] = jnp.concatenate(
+            numers + list(pack(by_block(peaks), by_block(totals))), axis=0
         ).astype(bf16)
 
     @pl.when(w >= 2)
     def _():
-        r3t[16] = jnp.where(low16, neg_large, 0.0)
-        r3n[16] = jnp.zeros((32, HD), bf16)
-
-    remote(r3t.at[pl.ds(0, 15)], r3t.at[pl.ds(0, 15)], 4, (s, w)).wait_recv()
-    remote(r3n.at[pl.ds(0, 15)], r3n.at[pl.ds(0, 15)], 3, (s, w)).wait_recv()
-
-    def merge(stats, numers):
-        peak = stats[0]
-        for t in stats[1:]:
+        r3[16] = jnp.concatenate(
+            [jnp.zeros((32, HD), f32)]
+            + list(pack(jnp.full((GROUP, HD), neg_large, f32), jnp.zeros((GROUP, HD), f32))),
+            axis=0,
+        ).astype(bf16)
+
+    remote(r3.at[pl.ds(0, 15)], r3.at[pl.ds(0, 15)], 3, (s, w)).wait_recv()
+
+    def merge(messages):
+        messages = [msg.astype(f32) for msg in messages]
+        high = [msg[32:40] for msg in messages]
+        peak = high[0]
+        for t in high[1:]:
             peak = jnp.maximum(peak, t)
         total = jnp.zeros((GROUP, HD), f32)
         acc = [jnp.zeros((GROUP, HD), f32) for _ in range(4)]
-        for t, n in zip(stats, numers):
+        for t, msg in zip(high, messages):
             f = jnp.exp(t - peak)
-            total = total + f * pltpu.roll(t, HD - 16, 1)
+            total = total + f * pltpu.roll(t + msg[40:48], HD - 16, 1)
             for i in range(4):
-                acc[i] = acc[i] + jnp.broadcast_to(f[:, 32 * i : 32 * i + 1], (GROUP, HD)) * n[
+                acc[i] = acc[i] + jnp.broadcast_to(f[:, 32 * i : 32 * i + 1], (GROUP, HD)) * msg[
                     i * GROUP : (i + 1) * GROUP
                 ]
         return peak, total, acc
 
-    peak, total, acc = merge(
-        [r3t[i] for i in range(17)],
-        [r3n[i].astype(f32) for i in range(17)],
-    )
-    s4t[...] = jnp.where(low16, peak, pltpu.roll(total, 16, 1))
-    s4n[...] = jnp.concatenate(acc, axis=0).astype(bf16)
+    peak, total, acc = merge([r3[i] for i in range(17)])
+    s4[...] = jnp.concatenate(acc + list(pack(peak, pltpu.roll(total, 16, 1))), axis=0).astype(bf16)
     for tw in wide_to:
-        remote(s4n, r4n.at[w], 5, (s, tw)).start()
-        remote(s4t, r4t.at[w], 6, (s, tw)).start()
-    r4n[w] = s4n[...]
-    r4t[w] = s4t[...]
+        remote(s4, r4.at[w], 5, (s, tw)).start()
+    r4[w] = s4[...]
     small[7].wait()
-    remote(r4t.at[pl.ds(0, 15)], r4t.at[pl.ds(0, 15)], 6, (s, w)).wait_recv()
-    remote(r4n.at[pl.ds(0, 15)], r4n.at[pl.ds(0, 15)], 5, (s, w)).wait_recv()
+    remote(r4.at[pl.ds(0, 15)], r4.at[pl.ds(0, 15)], 5, (s, w)).wait_recv()
     for c in range(2):
-        peak, total, acc = merge(
-            [r4t[2 * i + c] for i in range(8)], [r4n[2 * i + c].astype(f32) for i in range(8)]
-        )
+        peak, total, acc = merge([r4[2 * i + c] for i in range(8)])
         for i in range(4):
             den = jnp.broadcast_to(total[:, 32 * i : 32 * i + 1], (GROUP, HD))
             of[pl.ds((c * 4 + i) * GROUP, GROUP), :] = acc[i] / den
@@ -360,10 +373,8 @@
             remote(skv, rkv.at[w], 1, (s, t)).wait_send()
 
     remote(qall.at[pl.ds(0, 31)], qall.at[pl.ds(0, 31)], 2, (s, w)).wait_send()
-    remote(r3n.at[pl.ds(0, 15)], r3n.at[pl.ds(0, 15)], 3, (s, w)).wait_send()
-    remote(r3t.at[pl.ds(0, 15)], r3t.at[pl.ds(0, 15)], 4, (s, w)).wait_send()
-    remote(r4n.at[pl.ds(0, 15)], r4n.at[pl.ds(0, 15)], 5, (s, w)).wait_send()
-    remote(r4t.at[pl.ds(0, 15)], r4t.at[pl.ds(0, 15)], 6, (s, w)).wait_send()
+    remote(r3.at[pl.ds(0, 15)], r3.at[pl.ds(0, 15)], 3, (s, w)).wait_send()
+    remote(r4.at[pl.ds(0, 15)], r4.at[pl.ds(0, 15)], 5, (s, w)).wait_send()
     remote(r5.at[pl.ds(0, 7)], r5.at[pl.ds(0, 7)], 7, (s, w)).wait_send()
 
 
@@ -405,14 +416,10 @@
             vm((ROWS, HD), f32),
             vm((4, HEADS, BLOCK), f32),
             vm((4, HEADS, BLOCK), bf16),
-            vm((2, KVH, 32, HD), bf16),
-            vm((2, KVH, GROUP, HD), f32),
-            vm((17, 32, HD), bf16),
-            vm((17, GROUP, HD), f32),
-            vm((32, HD), bf16),
-            vm((GROUP, HD), f32),
-            vm((NWIDE, 32, HD), bf16),
-            vm((NWIDE, GROUP, HD), f32),
+            vm((2, KVH, 48, HD), bf16),
+            vm((17, 48, HD), bf16),
+            vm((48, HD), bf16),
+            vm((NWIDE, 48, HD), bf16),
             vm((HEADS, HD), f32),
             vm((ROWS, WIDTH), f32),
             vm((NSEQ, ROWS, WIDTH), f32),

time: 35.5 us -> 35.2 us (level)
  Pallas kernels: 34.5 us -> 34 us
    pallas_call x1, Pallas kernels: 34.5 us -> 34 us  [body(): pl.pallas_call(kernel, out_shape=pltpu.VMEM((ROWS, WIDTH), f32), in_specs...]
where the time goes in v3:
time: 35.2 us; the launch traced here: 34.6 us
  Pallas kernels  34 us (97%)
  local copies, waits for them, and re-layouts  0.6 us (2%)
    pallas_call x1, Pallas kernels, body(): pl.pallas_call(kernel, out_shape=pltpu.VMEM((ROWS, WIDTH), f32), in_specs...  34 us

profile of v3, /device:TPU:0, one launch (start us, length us, event | category | flops | bytes accessed | tf_op | source)
XLA Modules:
  0.0 34.6 jit_solution(12073723215813315985)
XLA Ops:
  0.0 34.0 %shard_map.109 = f32[8,320]{1,0:T(8,128)S(1)} custom-call(bf16[8,320]{1,0:T(8,128)(2,1)} %x_hbm.1, f32[320]{0:T(512)} %gain_hbm.1, bf16[320,1024]{1,0:T(8,128)(2,1)} %wq_hbm.1, bf16[640,128]{1,0:T(8,128)(2,1)} %bitcast.9, bf16[320,1024]{1,0:T(8,128)(2,1)} %bitcast.8, f32[1,128]{1,0:T(1,128)} %bitcast.10, f32[1,128]{1,0:T(1,128)} %bitcast.11, ...), custom_call_target="tpu_custom_call" | custom-call | tf_op jit(solution)/shard_map/pallas_call | solution.py:389
  34.0 0.6 %copy.13 = f32[8,320]{1,0:T(8,128)} copy(f32[8,320]{1,0:T(8,128)S(1)} %shard_map.109) | data formatting | bytes 20480

commit v4 on v3

--- a/solution.py
+++ b/solution.py
@@ -29,10 +29,10 @@
 
 
 def kernel(
-    x_hbm, gain_hbm, wq_hbm, wkv_hbm, wo_hbm, qg_hbm, kg_hbm, k_hbm, v_hbm, freq_hbm, len_ref,
+    x_hbm, gain_hbm, wq_hbm, wkv_hbm, wo_hbm, qg_hbm, kg_hbm, k_hbm, v_hbm, freq_hbm, len_hbm,
     out_ref,
     x_v, gain_v, wq_v, wkv_v, wo_v, qg_v, kg_v, k_v, v_v, freq_v,
-    k_t, v_r, s1, r1, skv, rkv, sq, qall, qf, qt, knew, vnew, scr, pb,
+    len_ref, k_t, v_r, s1, r1, skv, rkv, sq, qall, qf, qt, knew, vnew, scr, pb,
     s3, r3, s4, r4, of, s5, r5,
     in_sem, k_sem, v_sem, ssem, rsem,
 ):
@@ -56,11 +56,10 @@
                 (freq_hbm, freq_v),
                 (wkv_hbm, wkv_v),
                 (wo_hbm, wo_v),
+                (len_hbm, len_ref),
             ]
         )
     ]
-    for c in small[:6]:
-        c.start()
 
     def ring(k):
         return min(k, 4 - k)
@@ -96,6 +95,8 @@
     steps.sort(key=lambda k: -ring(k[0]) - k[1])
     seq_to = [((yl + lo) % 2) * 4 + (z + kz) % 4 for kz, lo in steps if kz or lo]
 
+    for c in small[:3]:
+        c.start()
     bar = pltpu.get_barrier_semaphore()
     n_bar = 0
     for tw in wide_to:
@@ -112,14 +113,14 @@
             device_id=to, device_id_type=MESH,
         )
 
-    for c in small[6:]:
+    for c in small[3:]:
         c.start()
     k_cp = [pltpu.make_async_copy(k_hbm.at[b], k_v.at[b], k_sem.at[b]) for b in range(ROWS)]
     v_cp = [pltpu.make_async_copy(v_hbm.at[b], v_v.at[b], v_sem.at[b]) for b in range(ROWS)]
     for c in k_cp + v_cp:
         c.start()
 
-    for c in small[:6]:
+    for c in small[:3]:
         c.wait()
     xf = x_v[...].astype(f32)
     ss = jnp.sum(xf * xf, axis=-1, keepdims=True)
@@ -152,7 +153,8 @@
     for tw in wide_to:
         remote(s1.at[tw % 4], r1.at[w], 0, (s, tw)).start()
 
-    small[6].wait()
+    for c in small[3:7]:
+        c.wait()
     row_i = lax.broadcasted_iota(jnp.int32, (WIDTH, 2 * WIDTH), 0)
     col_i = lax.broadcasted_iota(jnp.int32, (WIDTH, 2 * WIDTH), 1)
     spread = jnp.where(col_i // 2 == row_i, 1.0, 0.0).astype(bf16)
@@ -165,6 +167,7 @@
     skv[0] = kv_part[:ROWS]
     skv[1] = kv_part[ROWS:]
 
+    small[8].wait()
     lens = jnp.zeros((ROWS, HD), jnp.int32)
     for b in range(ROWS):
         lens = jnp.where(row == b, len_ref[b], lens)
@@ -389,7 +392,7 @@
     return pl.pallas_call(
         kernel,
         out_shape=pltpu.VMEM((ROWS, WIDTH), f32),
-        in_specs=[any_spec] * 10 + [pl.BlockSpec(memory_space=pltpu.SMEM)],
+        in_specs=[any_spec] * 11,
         out_specs=pl.BlockSpec(memory_space=pltpu.VMEM),
         scratch_shapes=[
             vm((ROWS, WIDTH), bf16),
@@ -402,6 +405,7 @@
             vm((ROWS, FLAT, HD), bf16),
             vm((ROWS, FLAT, HD), bf16),
             vm((1, HD), f32),
+            pltpu.SMEM((ROWS,), jnp.int32),
             vm((ROWS, KVH * HD, BLOCK), bf16),
             vm((ROWS, BLOCK, KVH * HD), bf16),
             vm((4, 17, HD), f32),
@@ -423,7 +427,7 @@
             vm((HEADS, HD), f32),
             vm((ROWS, WIDTH), f32),
             vm((NSEQ, ROWS, WIDTH), f32),
-            pltpu.SemaphoreType.DMA((8,)),
+            pltpu.SemaphoreType.DMA((9,)),
             pltpu.SemaphoreType.DMA((ROWS,)),
             pltpu.SemaphoreType.DMA((ROWS,)),
             pltpu.SemaphoreType.DMA((8,)),

time: 35.2 us -> 34.4 us (0.977)
  Pallas kernels: 34 us -> 33.3 us
    pallas_call x1, Pallas kernels: 34 us -> 33.3 us  [body(): pl.pallas_call(kernel, out_shape=pltpu.VMEM((ROWS, WIDTH), f32), in_specs...]
where the time goes in v4:
time: 34.4 us; the launch traced here: 33.9 us
  Pallas kernels  33.3 us (97%)
  local copies, waits for them, and re-layouts  0.6 us (2%)
    pallas_call x1, Pallas kernels, body(): pl.pallas_call(kernel, out_shape=pltpu.VMEM((ROWS, WIDTH), f32), in_specs...  33.3 us

profile of v4, /device:TPU:0, one launch (start us, length us, event | category | flops | bytes accessed | tf_op | source)
XLA Modules:
  0.0 33.9 jit_solution(3728680216421462076)
XLA Ops:
  0.0 33.3 %shard_map.109 = f32[8,320]{1,0:T(8,128)S(1)} custom-call(bf16[8,320]{1,0:T(8,128)(2,1)} %x_hbm.1, f32[320]{0:T(512)} %gain_hbm.1, bf16[320,1024]{1,0:T(8,128)(2,1)} %wq_hbm.1, bf16[640,128]{1,0:T(8,128)(2,1)} %bitcast.9, bf16[320,1024]{1,0:T(8,128)(2,1)} %bitcast.8, f32[1,128]{1,0:T(1,128)} %bitcast.10, f32[1,128]{1,0:T(1,128)} %bitcast.11, ...), custom_call_target="tpu_custom_call" | custom-call | tf_op jit(solution)/shard_map/pallas_call | solution.py:392
  33.3 0.6 %copy.13 = f32[8,320]{1,0:T(8,128)} copy(f32[8,320]{1,0:T(8,128)S(1)} %shard_map.109) | data formatting | bytes 20480

commit v5 on v4

--- a/solution.py
+++ b/solution.py
@@ -239,10 +239,11 @@
         return jnp.where(n, peak, high), jnp.where(n, 0.0, total - high)
 
     slot3 = s * 2 + core
-    for c in range(2):
-        rows = range(c * 4, c * 4 + 4)
+    def half(c, carry):
+        c = (core + c) % 2
+        rows = [c * 4 + i for i in range(4)]
         scores, peaks, totals, weights, numers = {}, {}, {}, {}, {}
-        for b in rows:
+        for i, b in enumerate(rows):
             parts = []
             for pr in range(4):
                 one = qt[b, 16 * pr : 16 * pr + 8, :]
@@ -253,29 +254,29 @@
                 ).astype(bf16)
                 keys = k_t[b, pr * 256 : (pr + 1) * 256, :]
                 parts.append(jnp.dot(lhs, keys, preferred_element_type=f32))
-            scr[b % 4] = jnp.concatenate(parts, axis=0)
-        for b in rows:
+            scr[i] = jnp.concatenate(parts, axis=0)
+        for i, b in enumerate(rows):
             valid = plane < len_ref[b] - start
-            t = jnp.where(valid, scr[b % 4] * scale, neg_large)
+            t = jnp.where(valid, scr[i] * scale, neg_large)
             m = jnp.max(t, axis=-1, keepdims=True).astype(bf16).astype(f32)
             e = jnp.where(valid, jnp.exp(t - m), 0.0)
-            peaks[b] = jnp.broadcast_to(m, (HEADS, HD))
-            totals[b] = jnp.broadcast_to(jnp.sum(e, axis=-1, keepdims=True), (HEADS, HD))
-            pb[b % 4] = e.astype(bf16)
-        for b in rows:
+            peaks[i] = jnp.broadcast_to(m, (HEADS, HD))
+            totals[i] = jnp.broadcast_to(jnp.sum(e, axis=-1, keepdims=True), (HEADS, HD))
+            pb[i] = e.astype(bf16)
+        for i, b in enumerate(rows):
             for pr in range(4):
                 n = jnp.dot(
-                    pb[b % 4, 16 * pr : 16 * pr + 16, :],
+                    pb[i, 16 * pr : 16 * pr + 16, :],
                     v_r[b, :, pr * 256 : (pr + 1) * 256],
                     preferred_element_type=f32,
                 )
-                numers[b, 2 * pr] = n[:GROUP, :HD]
-                numers[b, 2 * pr + 1] = n[GROUP:, HD:]
-        stats = pack(by_block([peaks[b] for b in rows]), by_block([totals[b] for b in rows]))
+                numers[i, 2 * pr] = n[:GROUP, :HD]
+                numers[i, 2 * pr + 1] = n[GROUP:, HD:]
+        stats = pack(by_block([peaks[i] for i in range(4)]), by_block([totals[i] for i in range(4)]))
         for g in range(KVH):
             own = slice(g * GROUP, (g + 1) * GROUP)
             s3[c, g] = jnp.concatenate(
-                [numers[b, g] for b in rows] + [part[own] for part in stats], axis=0
+                [numers[i, g] for i in range(4)] + [part[own] for part in stats], axis=0
             ).astype(bf16)
         tw = w - core + c
         for ts in seq_to:
@@ -288,6 +289,10 @@
         @pl.when(core == c)
         def _():
             r3[slot3] = s3[c, s]
+        return carry
+
+    half(0, 0)
+    half(1, 0)
 
     @pl.when(w < 2)
     def _():

time: 34.4 us -> 34.5 us (level); the launches traced: 33.9 us -> 34.4 us
  Pallas kernels: 33.3 us -> 33.8 us
    pallas_call x1, Pallas kernels: 33.3 us -> 33.8 us  [body(): pl.pallas_call(kernel, out_shape=pltpu.VMEM((ROWS, WIDTH), f32), in_specs...]
where the time goes in v5:
time: 34.5 us; the launch traced here: 34.4 us
  Pallas kernels  33.8 us (98%)
  local copies, waits for them, and re-layouts  0.6 us (2%)
    pallas_call x1, Pallas kernels, body(): pl.pallas_call(kernel, out_shape=pltpu.VMEM((ROWS, WIDTH), f32), in_specs...  33.8 us

profile of v5, /device:TPU:0, one launch (start us, length us, event | category | flops | bytes accessed | tf_op | source)
XLA Modules:
  0.0 34.4 jit_solution(2237850707054061167)
XLA Ops:
  0.0 33.8 %shard_map.109 = f32[8,320]{1,0:T(8,128)S(1)} custom-call(bf16[8,320]{1,0:T(8,128)(2,1)} %x_hbm.1, f32[320]{0:T(512)} %gain_hbm.1, bf16[320,1024]{1,0:T(8,128)(2,1)} %wq_hbm.1, bf16[640,128]{1,0:T(8,128)(2,1)} %bitcast.9, bf16[320,1024]{1,0:T(8,128)(2,1)} %bitcast.8, f32[1,128]{1,0:T(1,128)} %bitcast.10, f32[1,128]{1,0:T(1,128)} %bitcast.11, ...), custom_call_target="tpu_custom_call" | custom-call | tf_op jit(solution)/shard_map/pallas_call | solution.py:397
  33.8 0.6 %copy.13 = f32[8,320]{1,0:T(8,128)} copy(f32[8,320]{1,0:T(8,128)S(1)} %shard_map.109) | data formatting | bytes 20480
